TPU v7x, 32 devices: a whole 2x2x4 slice. The times are simulated.
32 devices in a mesh: head: 4 (over y, x), inner: 4 (over z), outer: 2 (over core).
Axes of the slice: x: 2, y: 2, z: 4, core: 2. Of those that a mesh axis runs over, the one named last changes fastest.
Arguments:
- queries: bfloat16 [2, 4096, 4096], P('outer', ('head', 'inner')), may hold values from -5 to 5
- key_states: bfloat16 [2, 4096, 4096], P('outer', ('head', 'inner')), may hold values from -5 to 5
- value_states: bfloat16 [2, 4096, 4096], P('outer', ('head', 'inner')), may hold values from -6 to 6
- out_grad: bfloat16 [2, 4096, 4096], P('outer', ('head', 'inner')), may hold values from -6 to 6
- positions: int32 [2, 4096], replicated, may hold values from 0 to 8191, as said below
- doc_start: int32 [2, 4096], replicated, may hold values from 0 to 8191, as said below
Outputs:
- attended: bfloat16 [2, 4096, 4096], P('outer', ('head', 'inner'))
- query_grad: bfloat16 [2, 4096, 4096], P('outer', ('head', 'inner'))
- key_grad: bfloat16 [2, 4096, 4096], P('outer', ('head', 'inner'))
- value_grad: bfloat16 [2, 4096, 4096], P('outer', ('head', 'inner'))
Inputs may be any that keep to these rules, and one draw needn't show every extreme that they name: The 8192 positions form 2 * 2 blocks of 2048 consecutive positions; each half of a context rank's 4096 rows holds one whole block in rising order, and which rank and half holds which block varies. The sequence is cut into documents of consecutive positions, each at most 512 positions long and one exactly 512; doc_start is the first position of the token's document.
All inputs are finite; a program needn't handle non-finite values.
Results may differ from a plain program's by a relative error of at most 0.023.
Values may be sent and summed in bfloat16 or wider, within the bound.
A program may use at most 192 MiB of HBM per device.

v0:
```python
import jax
import jax.numpy as jnp
from jax import lax
from jax.sharding import PartitionSpec as P

DH = 128
DOC_MOST = 512


neg_large = -1e30


def to_halves(array, head_count):
    total_rows = array.shape[1]
    return array.reshape(2, total_rows // 2, head_count, DH).transpose(0, 2, 1, 3)


def from_halves(array):
    halves, heads_here, half_rows, depth = array.shape
    return array.transpose(0, 2, 1, 3).reshape(1, halves * half_rows, heads_here * depth)


def visible_pairs(query_pos, query_first, key_pos):
    return (key_pos[:, None, :] <= query_pos[:, :, None]) & (
        key_pos[:, None, :] >= query_first[:, :, None]
    )


def scaled_scores(query_part, key_part, visible):
    raw = jnp.einsum(
        "shqd,shkd->shqk", query_part, key_part, preferred_element_type=jnp.float32
    ) * DH ** (-0.5)
    return jnp.where(visible[:, None], raw, neg_large)


def slot_of(span_ids, wanted):
    slot_ids = jnp.arange(span_ids.shape[0], dtype=jnp.int32)
    return jnp.sum(jnp.where(span_ids[None, :] == wanted[:, None], slot_ids[None, :], 0), axis=1)


def body(queries, key_states, value_states, out_grad, positions, doc_start):
    query_here, key_here, value_here, grad_here = (
        lax.all_to_all(queries, ("head", "inner"), split_axis=2, concat_axis=1, tiled=True),
        lax.all_to_all(key_states, ("head", "inner"), split_axis=2, concat_axis=1, tiled=True),
        lax.all_to_all(value_states, ("head", "inner"), split_axis=2, concat_axis=1, tiled=True),
        lax.all_to_all(out_grad, ("head", "inner"), split_axis=2, concat_axis=1, tiled=True),
    )
    head_count = query_here.shape[2] // DH
    query_h = to_halves(query_here, head_count)
    key_h = to_halves(key_here, head_count)
    value_h = to_halves(value_here, head_count)
    grad_h = to_halves(grad_here, head_count)
    half_rows = query_h.shape[2]
    block_rows = min(512, half_rows)
    window = DOC_MOST + block_rows
    span_total = 2 * positions.shape[0]
    pos_table = positions.reshape(span_total, half_rows)
    first_table = doc_start.reshape(span_total, half_rows)
    span_ids = pos_table[:, 0] // half_rows
    own_rank = lax.axis_index("outer")
    own_slots = own_rank * 2 + jnp.arange(2, dtype=jnp.int32)
    own_pos = jnp.take(pos_table, own_slots, axis=0)
    own_first = jnp.take(first_table, own_slots, axis=0)
    span_here = jnp.take(span_ids, own_slots)
    tail_keys = key_h[:, :, half_rows - DOC_MOST :]
    tail_values = value_h[:, :, half_rows - DOC_MOST :]
    head_queries = query_h[:, :, :DOC_MOST]
    head_grads = grad_h[:, :, :DOC_MOST]
    keys_far, values_far = (
        lax.all_gather(tail_keys, "outer", axis=0, tiled=True),
        lax.all_gather(tail_values, "outer", axis=0, tiled=True),
    )
    prev_slots = slot_of(span_ids, span_here - 1)
    ext_keys = jnp.concatenate([jnp.take(keys_far, prev_slots, axis=0), key_h], axis=2)
    ext_values = jnp.concatenate([jnp.take(values_far, prev_slots, axis=0), value_h], axis=2)
    near_rows = jnp.arange(DOC_MOST, dtype=jnp.int32)
    ext_pos = jnp.concatenate(
        [span_here[:, None] * half_rows - DOC_MOST + near_rows[None, :], own_pos], axis=1
    )
    key_acc = jnp.zeros((2, head_count, half_rows, DH), jnp.float32)
    value_acc = jnp.zeros((2, head_count, half_rows, DH), jnp.float32)
    attended_pieces = []
    query_pieces = []
    log_pieces = []
    delta_pieces = []
    for block_index in range(half_rows // block_rows):
        lower_row = block_index * block_rows
        query_part = query_h[:, :, lower_row : lower_row + block_rows]
        grad_part = grad_h[:, :, lower_row : lower_row + block_rows]
        key_part = ext_keys[:, :, lower_row : lower_row + window]
        value_part = ext_values[:, :, lower_row : lower_row + window]
        visible = visible_pairs(
            own_pos[:, lower_row : lower_row + block_rows],
            own_first[:, lower_row : lower_row + block_rows],
            ext_pos[:, lower_row : lower_row + window],
        )
        scores = scaled_scores(query_part, key_part, visible)
        top_score = jnp.max(scores, axis=3)
        mass_sum = jnp.sum(
            jnp.where(visible[:, None], jnp.exp(scores - top_score[..., None]), 0.0), axis=3
        )
        log_total = top_score + jnp.log(mass_sum)
        weights = jnp.where(visible[:, None], jnp.exp(scores - log_total[..., None]), 0.0)
        weights_low = weights.astype(jnp.bfloat16)
        attended_part = jnp.einsum(
            "shqk,shkd->shqd", weights_low, value_part, preferred_element_type=jnp.float32
        ).astype(jnp.bfloat16)
        row_delta = jnp.sum(
            attended_part.astype(jnp.float32) * grad_part.astype(jnp.float32), axis=3
        )
        prob_grad = jnp.einsum(
            "shqd,shkd->shqk", grad_part, value_part, preferred_element_type=jnp.float32
        )
        score_grad = (weights * (prob_grad - row_delta[..., None]) * DH ** (-0.5)).astype(
            jnp.bfloat16
        )
        query_pieces.append(
            jnp.einsum(
                "shqk,shkd->shqd", score_grad, key_part, preferred_element_type=jnp.float32
            ).astype(jnp.bfloat16)
        )
        own_col = max(DOC_MOST - lower_row, 0)
        row_start = lower_row + own_col - DOC_MOST
        row_end = lower_row + block_rows
        key_acc = key_acc.at[:, :, row_start:row_end].add(
            jnp.einsum(
                "shqk,shqd->shkd",
                score_grad[..., own_col:],
                query_part,
                preferred_element_type=jnp.float32,
            )
        )
        value_acc = value_acc.at[:, :, row_start:row_end].add(
            jnp.einsum(
                "shqk,shqd->shkd",
                weights_low[..., own_col:],
                grad_part,
                preferred_element_type=jnp.float32,
            )
        )
        attended_pieces.append(attended_part)
        log_pieces.append(log_total)
        delta_pieces.append(row_delta)
    attended = jnp.concatenate(attended_pieces, axis=2)
    query_grad = from_halves(jnp.concatenate(query_pieces, axis=2))
    log_all = jnp.concatenate(log_pieces, axis=2)
    delta_all = jnp.concatenate(delta_pieces, axis=2)
    log_far, delta_far = (
        lax.all_gather(log_all[:, :, :DOC_MOST], "outer", axis=0, tiled=True),
        lax.all_gather(delta_all[:, :, :DOC_MOST], "outer", axis=0, tiled=True),
    )
    queries_far, grads_far = (
        lax.all_gather(head_queries, "outer", axis=0, tiled=True),
        lax.all_gather(head_grads, "outer", axis=0, tiled=True),
    )
    next_slots = slot_of(span_ids, span_here + 1)
    has_next = span_here + 1 < span_total
    query_next = jnp.take(queries_far, next_slots, axis=0)
    grad_next = jnp.take(grads_far, next_slots, axis=0)
    log_next = jnp.take(log_far, next_slots, axis=0)
    delta_next = jnp.take(delta_far, next_slots, axis=0)
    pos_next = jnp.take(pos_table, next_slots, axis=0)[:, :DOC_MOST]
    first_next = jnp.take(first_table, next_slots, axis=0)[:, :DOC_MOST]
    visible = (
        visible_pairs(pos_next, first_next, own_pos[:, half_rows - DOC_MOST :])
        & has_next[:, None, None]
    )
    scores = scaled_scores(query_next, tail_keys, visible)
    weights = jnp.where(visible[:, None], jnp.exp(scores - log_next[..., None]), 0.0)
    weights_low = weights.astype(jnp.bfloat16)
    value_acc = value_acc.at[:, :, half_rows - DOC_MOST :].add(
        jnp.einsum("shqk,shqd->shkd", weights_low, grad_next, preferred_element_type=jnp.float32)
    )
    prob_grad = jnp.einsum(
        "shqd,shkd->shqk", grad_next, tail_values, preferred_element_type=jnp.float32
    )
    score_grad = (weights * (prob_grad - delta_next[..., None]) * DH ** (-0.5)).astype(jnp.bfloat16)
    key_acc = key_acc.at[:, :, half_rows - DOC_MOST :].add(
        jnp.einsum("shqk,shqd->shkd", score_grad, query_next, preferred_element_type=jnp.float32)
    )
    key_grad = from_halves(key_acc.astype(jnp.bfloat16))
    value_grad = from_halves(value_acc.astype(jnp.bfloat16))
    attended_home, query_home, key_home, value_home = (
        lax.all_to_all(
            from_halves(attended), ("head", "inner"), split_axis=1, concat_axis=2, tiled=True
        ),
        lax.all_to_all(query_grad, ("head", "inner"), split_axis=1, concat_axis=2, tiled=True),
        lax.all_to_all(key_grad, ("head", "inner"), split_axis=1, concat_axis=2, tiled=True),
        lax.all_to_all(value_grad, ("head", "inner"), split_axis=1, concat_axis=2, tiled=True),
    )
    return (attended_home, query_home, key_home, value_home)


def solution(mesh):
    return jax.shard_map(
        body,
        mesh=mesh,
        in_specs=(
            P("outer", ("head", "inner"), None),
            P("outer", ("head", "inner"), None),
            P("outer", ("head", "inner"), None),
            P("outer", ("head", "inner"), None),
            P(),
            P(),
        ),
        out_specs=(
            P("outer", ("head", "inner"), None),
            P("outer", ("head", "inner"), None),
            P("outer", ("head", "inner"), None),
            P("outer", ("head", "inner"), None),
        ),
        check_vma=False,
    )
```

profile of v0, /device:TPU:0, one launch (start us, length us, event | category | flops | bytes accessed | tf_op | source)
XLA Modules:
  0.0 841.9 jit_solution(17862047002944975533)
XLA Ops:
  17.8 21.6 %reduce.23 = bf16[4096,256]{1,0:T(8,128)(2,1)S(1)} reduce(bf16[4096,1,256]{2,1,0:T(2,128)(2,1)} %bitcast.108, bf16[]{:T(256)} %broadcast.634), dimensions={1}, to_apply=%bitcast.72.reduce_sub_computation | reduce | bytes 4194306
  59.7 22.9 %reduce.22 = bf16[4096,256]{1,0:T(8,128)(2,1)} reduce(bf16[4096,1,256]{2,1,0:T(2,128)(2,1)} %bitcast.121, bf16[]{:T(256)} %broadcast.634), dimensions={1}, to_apply=%bitcast.70.reduce_sub_computation | reduce | bytes 4194306
  86.6 13.0 %all-to-all-done = bf16[16,2,32768]{2,1,0:T(2,128)(2,1)S(1)} async-done(((bf16[16,2,32768]{2,1,0:T(2,128)(2,1)}), bf16[16,2,32768]{2,1,0:T(2,128)(2,1)S(1)}, u32[]{:S(2)}, u32[]{:S(2)}) %all-to-all-start) | async-done | bytes 2097184 | tf_op jit(solution)/shard_map/all_to_all | solution.py:44
  114.7 22.9 %reduce.24 = bf16[4096,256]{1,0:T(8,128)(2,1)} reduce(bf16[4096,1,256]{2,1,0:T(2,128)(2,1)} %bitcast.122, bf16[]{:T(256)} %broadcast.634), dimensions={1}, to_apply=%bitcast.74.reduce_sub_computation | reduce | bytes 4194306
  141.6 12.5 %all-to-all-done.2 = bf16[16,2,32768]{2,1,0:T(2,128)(2,1)S(1)} async-done(((bf16[16,2,32768]{2,1,0:T(2,128)(2,1)}), bf16[16,2,32768]{2,1,0:T(2,128)(2,1)S(1)}, u32[]{:S(2)}, u32[]{:S(2)}) %all-to-all-start.2) | async-done | bytes 2097184 | tf_op jit(solution)/shard_map/all_to_all | solution.py:45
  172.4 21.6 %reduce.25 = bf16[4096,256]{1,0:T(8,128)(2,1)S(1)} reduce(bf16[4096,1,256]{2,1,0:T(2,128)(2,1)} %bitcast.123, bf16[]{:T(256)} %broadcast.634), dimensions={1}, to_apply=%bitcast.78.reduce_sub_computation | reduce | bytes 4194306
  196.1 12.2 %all-to-all-done.1 = bf16[16,2,32768]{2,1,0:T(2,128)(2,1)} async-done(((bf16[16,2,32768]{2,1,0:T(2,128)(2,1)}), bf16[16,2,32768]{2,1,0:T(2,128)(2,1)}, u32[]{:S(2)}, u32[]{:S(2)}) %all-to-all-start.1) | async-done | bytes 2097184 | tf_op jit(solution)/shard_map/all_to_all | solution.py:43
  239.1 11.0 %reshape.676 = bf16[4096,1,256]{2,1,0:T(2,128)(2,1)} reshape(bf16[16,2,32768]{2,1,0:T(2,128)(2,1)} %copy-done.4) | data formatting | bytes 4194304
  265.8 10.4 %reshape.680 = bf16[4096,1,256]{2,1,0:T(2,128)(2,1)} reshape(bf16[16,2,32768]{2,1,0:T(2,128)(2,1)} %all-to-all-done.1) | data formatting | bytes 4194304
  291.1 10.4 %reshape.684 = bf16[4096,1,256]{2,1,0:T(2,128)(2,1)} reshape(bf16[16,2,32768]{2,1,0:T(2,128)(2,1)} %all-to-all-done.4) | data formatting | bytes 4194304
  443.5 18.1 %copy.215 = bf16[2,2048,2,128]{3,2,1,0:T(2,128)(2,1)} copy(bf16[2,2048,2,128]{3,1,2,0:T(8,128)(2,1)S(1)} %convert_bitcast_fusion) | data formatting | bytes 4194304 | tf_op jit(solution)/shard_map/transpose | solution.py:20
  461.7 13.6 %reshape.673 = bf16[1,4096,256]{2,0,1:T(2,128)(2,1)} reshape(bf16[2,2048,2,128]{3,2,1,0:T(2,128)(2,1)} %copy.215) | data formatting | bytes 4194304 | tf_op jit(solution)/shard_map/reshape | solution.py:20
  475.2 23.1 %reduce.29 = bf16[4096,256]{1,0:T(8,128)(2,1)} reduce(bf16[4096,1,256]{2,1,0:T(2,128)(2,1)} %bitcast.114, bf16[]{:T(256)} %broadcast.634), dimensions={1}, to_apply=%bitcast.84.reduce_sub_computation | reduce | bytes 4194306
  555.5 18.1 %copy.211 = bf16[2,2048,2,128]{3,2,1,0:T(2,128)(2,1)} copy(bf16[2,2048,2,128]{3,1,2,0:T(8,128)(2,1)S(1)} %convert_bitcast_fusion.1) | data formatting | bytes 4194304 | tf_op jit(solution)/shard_map/transpose | solution.py:20
  573.6 13.5 %reshape.672 = bf16[1,4096,256]{2,0,1:T(2,128)(2,1)} reshape(bf16[2,2048,2,128]{3,2,1,0:T(2,128)(2,1)} %copy.211) | data formatting | bytes 4194304 | tf_op jit(solution)/shard_map/reshape | solution.py:20
  587.1 22.9 %reduce.28 = bf16[4096,256]{1,0:T(8,128)(2,1)} reduce(bf16[4096,1,256]{2,1,0:T(2,128)(2,1)} %bitcast.115, bf16[]{:T(256)} %broadcast.634), dimensions={1}, to_apply=%bitcast.82.reduce_sub_computation | reduce | bytes 4194306
  631.3 20.0 %copy.207 = bf16[2,2048,2,128]{3,2,1,0:T(2,128)(2,1)S(1)} copy(bf16[2,2048,2,128]{3,1,2,0:T(8,128)(2,1)S(1)} %maximum_bitcast_fusion.1) | data formatting | bytes 4194304 | tf_op jit(solution)/shard_map/transpose | solution.py:20
  657.4 21.6 %reduce.27 = bf16[4096,256]{1,0:T(8,128)(2,1)S(1)} reduce(bf16[4096,1,256]{2,1,0:T(2,128)(2,1)} %bitcast.116, bf16[]{:T(256)} %broadcast.634), dimensions={1}, to_apply=%bitcast.80.reduce_sub_computation | reduce | bytes 4194306
  689.7 18.1 %copy.194 = bf16[2,2048,2,128]{3,2,1,0:T(2,128)(2,1)} copy(bf16[2,2048,2,128]{3,1,2,0:T(8,128)(2,1)S(1)} %maximum_bitcast_fusion) | data formatting | bytes 4194304 | tf_op jit(solution)/shard_map/transpose | solution.py:20
  707.8 13.5 %reshape.670 = bf16[1,4096,256]{2,0,1:T(2,128)(2,1)} reshape(bf16[2,2048,2,128]{3,2,1,0:T(2,128)(2,1)} %copy.194) | data formatting | bytes 4194304 | tf_op jit(solution)/shard_map/reshape | solution.py:20
  721.3 22.9 %reduce.26 = bf16[4096,256]{1,0:T(8,128)(2,1)} reduce(bf16[4096,1,256]{2,1,0:T(2,128)(2,1)} %bitcast.109, bf16[]{:T(256)} %broadcast.634), dimensions={1}, to_apply=%bitcast.76.reduce_sub_computation | reduce | bytes 4194306
  755.5 10.4 %reshape.690 = bf16[4096,1,256]{2,1,0:T(2,128)(2,1)} reshape(bf16[16,2,32768]{2,1,0:T(2,128)(2,1)} %all-to-all-done.7) | data formatting | bytes 4194304
  777.8 10.4 %reshape.688 = bf16[4096,1,256]{2,1,0:T(2,128)(2,1)} reshape(bf16[16,2,32768]{2,1,0:T(2,128)(2,1)} %all-to-all-done.6) | data formatting | bytes 4194304
  815.7 10.4 %reshape.682 = bf16[4096,1,256]{2,1,0:T(2,128)(2,1)} reshape(bf16[16,2,32768]{2,1,0:T(2,128)(2,1)} %all-to-all-done.3) | data formatting | bytes 4194304
  (268 shorter events, 431.4 us)
Async XLA Ops:
  41.4 58.3 %all-to-all-start = ((bf16[16,2,32768]{2,1,0:T(2,128)(2,1)}), bf16[16,2,32768]{2,1,0:T(2,128)(2,1)S(1)}, u32[]{:S(2)}, u32[]{:S(2)}) async-start(bf16[16,2,32768]{2,1,0:T(2,128)(2,1)} %reshape.677), calls=%async_computation | async-start | bytes 4194304 | tf_op jit(solution)/shard_map/all_to_all | solution.py:44
  101.0 53.1 %all-to-all-start.2 = ((bf16[16,2,32768]{2,1,0:T(2,128)(2,1)}), bf16[16,2,32768]{2,1,0:T(2,128)(2,1)S(1)}, u32[]{:S(2)}, u32[]{:S(2)}) async-start(bf16[16,2,32768]{2,1,0:T(2,128)(2,1)} %reshape.675), calls=%async_computation.2 | async-start | bytes 4194304 | tf_op jit(solution)/shard_map/all_to_all | solution.py:45
  137.7 21.2 %copy-start.43 = (s32[2,4096]{1,0:T(2,128)S(1)}, s32[2,4096]{1,0:T(2,128)}, u32[]{:S(2)}) copy-start(s32[2,4096]{1,0:T(2,128)} %param.36) | copy-start | bytes 98308
  137.7 21.2 %copy-start.44 = (s32[2,4096]{1,0:T(2,128)S(1)}, s32[2,4096]{1,0:T(2,128)}, u32[]{:S(2)}) copy-start(s32[2,4096]{1,0:T(2,128)} %param.37) | copy-start | bytes 98308
  154.1 54.1 %all-to-all-start.1 = ((bf16[16,2,32768]{2,1,0:T(2,128)(2,1)}), bf16[16,2,32768]{2,1,0:T(2,128)(2,1)}, u32[]{:S(2)}, u32[]{:S(2)}) async-start(bf16[16,2,32768]{2,1,0:T(2,128)(2,1)} %reshape.679), calls=%async_computation.1 | async-start | bytes 4194304 | tf_op jit(solution)/shard_map/all_to_all | solution.py:43
  196.1 24.7 %copy-start.6 = (bf16[16,2,32768]{2,1,0:T(2,128)(2,1)S(1)}, bf16[16,2,32768]{2,1,0:T(2,128)(2,1)}, u32[]{:S(2)}) copy-start(bf16[16,2,32768]{2,1,0:T(2,128)(2,1)} %copy-done.5) | copy-start | bytes 6291460
  208.2 82.9 %all-to-all-start.4 = ((bf16[16,2,32768]{2,1,0:T(2,128)(2,1)}), bf16[16,2,32768]{2,1,0:T(2,128)(2,1)}, u32[]{:S(2)}, u32[]{:S(2)}) async-start(bf16[16,2,32768]{2,1,0:T(2,128)(2,1)} %reshape.683), calls=%async_computation.4 | async-start | bytes 4194304 | tf_op jit(solution)/shard_map/all_to_all | solution.py:46
  212.7 159.4 %all-gather.5.cloned.1.call-start = ((), (), s32[]{:S(2)}) async-start(), calls=%async_computation.8 | async-start | bytes 1572864 | tf_op jit(solution)/shard_map/all_gather | solution.py:70
  239.0 135.7 %all-gather.7.cloned.1.call-start = ((), (), s32[]{:S(2)}) async-start(), calls=%async_computation.9 | async-start | bytes 1572864 | tf_op jit(solution)/shard_map/all_gather | solution.py:71
  348.5 69.9 %all-gather.9.cloned.1.call-start = ((), (), s32[]{:S(2)}) async-start(), calls=%async_computation.10 | async-start | bytes 1572864 | tf_op jit(solution)/shard_map/all_gather | solution.py:153
  348.8 10.1 %slice-start.4 = ((s8[8388608]{0:T(1024)(128)(4,1)}), s8[4194304]{0:T(1024)(128)(4,1)S(1)}, s32[]{:S(2)}) async-start(s8[8388608]{0:T(1024)(128)(4,1)} %bitcast.145), calls=%async_computation.16 | async-start | bytes 8388608
  364.0 69.5 %all-gather.11.cloned.1.call-start = ((), (), s32[]{:S(2)}) async-start(), calls=%async_computation.11 | async-start | bytes 1572864 | tf_op jit(solution)/shard_map/all_gather | solution.py:154
  382.7 10.9 %slice-start.6 = ((s8[8388608]{0:T(1024)(128)(4,1)}), s8[4194304]{0:T(1024)(128)(4,1)S(1)}, s32[]{:S(2)}) async-start(s8[8388608]{0:T(1024)(128)(4,1)} %bitcast.147), calls=%async_computation.18 | async-start | bytes 8388608
  393.6 9.8 %slice-start = ((s8[8388608]{0:T(1024)(128)(4,1)}), s8[4194304]{0:T(1024)(128)(4,1)S(1)}, s32[]{:S(2)}) async-start(s8[8388608]{0:T(1024)(128)(4,1)} %bitcast.141), calls=%async_computation.12 | async-start | bytes 8388608
  498.3 11.0 %copy-start.19 = (pred[2,512,1024]{1,2,0:T(8,128)(4,1)S(1)}, pred[2,512,1024]{1,2,0:T(8,128)(4,1)}, u32[]{:S(2)}) copy-start(pred[2,512,1024]{1,2,0:T(8,128)(4,1)} %compare_and_fusion.2) | copy-start | bytes 3145732
  502.4 111.6 %all-to-all-start.7 = ((bf16[16,2,32768]{2,1,0:T(2,128)(2,1)}), bf16[16,2,32768]{2,1,0:T(2,128)(2,1)}, u32[]{:S(2)}, u32[]{:S(2)}) async-start(bf16[16,2,32768]{2,1,0:T(2,128)(2,1)} %reshape.689), calls=%async_computation.7 | async-start | bytes 4194304 | tf_op jit(solution)/shard_map/all_to_all | solution.py:189
  516.8 10.7 %copy-start.24 = (bf16[2,2,512,1024]{2,3,1,0:T(8,128)(2,1)}, bf16[2,2,512,1024]{2,3,1,0:T(8,128)(2,1)S(1)}, u32[]{:S(2)}) copy-start(bf16[2,2,512,1024]{2,3,1,0:T(8,128)(2,1)S(1)} %multiply_convert_fusion.2) | copy-start | bytes 12582916
  527.5 8.7 %slice-start.2 = ((s8[8388608]{0:T(1024)(128)(4,1)}), s8[4194304]{0:T(1024)(128)(4,1)S(1)}, s32[]{:S(2)}) async-start(s8[8388608]{0:T(1024)(128)(4,1)} %bitcast.143), calls=%async_computation.14 | async-start | bytes 8388608
  610.0 11.1 %copy-start.9 = (bf16[2,2,512,128]{3,2,1,0:T(8,128)(2,1)S(1)}, bf16[2,2,512,128]{3,2,1,0:T(8,128)(2,1)}, u32[]{:S(2)}) copy-start(bf16[2,2,512,128]{3,2,1,0:T(8,128)(2,1)} %copy-done.8) | copy-start | bytes 1572868
  614.0 67.0 %all-to-all-start.6 = ((bf16[16,2,32768]{2,1,0:T(2,128)(2,1)}), bf16[16,2,32768]{2,1,0:T(2,128)(2,1)}, u32[]{:S(2)}, u32[]{:S(2)}) async-start(bf16[16,2,32768]{2,1,0:T(2,128)(2,1)} %reshape.687), calls=%async_computation.6 | async-start | bytes 4194304 | tf_op jit(solution)/shard_map/all_to_all | solution.py:188
  679.0 9.3 %copy-start.41 = (bf16[2,2,512,128]{3,2,1,0:T(8,128)(2,1)S(1)}, bf16[2,2,512,128]{3,2,1,0:T(8,128)(2,1)}, u32[]{:S(2)}) copy-start(bf16[2,2,512,128]{3,2,1,0:T(8,128)(2,1)} %convolution_convert_fusion.6) | copy-start | bytes 1572868
  679.0 9.3 %copy-start.42 = (bf16[2,2,512,128]{3,2,1,0:T(8,128)(2,1)S(1)}, bf16[2,2,512,128]{3,2,1,0:T(8,128)(2,1)}, u32[]{:S(2)}) copy-start(bf16[2,2,512,128]{3,2,1,0:T(8,128)(2,1)} %convolution_convert_fusion.5) | copy-start | bytes 1572868
  681.1 67.1 %all-to-all-start.5 = ((bf16[16,2,32768]{2,1,0:T(2,128)(2,1)}), bf16[16,2,32768]{2,1,0:T(2,128)(2,1)S(1)}, u32[]{:S(2)}, u32[]{:S(2)}) async-start(bf16[16,2,32768]{2,1,0:T(2,128)(2,1)} %reshape.685), calls=%async_computation.5 | async-start | bytes 4194304 | tf_op jit(solution)/shard_map/all_to_all | solution.py:187
  748.2 67.5 %all-to-all-start.3 = ((bf16[16,2,32768]{2,1,0:T(2,128)(2,1)}), bf16[16,2,32768]{2,1,0:T(2,128)(2,1)}, u32[]{:S(2)}, u32[]{:S(2)}) async-start(bf16[16,2,32768]{2,1,0:T(2,128)(2,1)} %reshape.681), calls=%async_computation.3 | async-start | bytes 4194304 | tf_op jit(solution)/shard_map/all_to_all | solution.py:184
  (41 other events, 213.9 us)
Sparse Core Ops, SparseCore 0:
  239.2 10.2 all-gather.4
  348.7 10.2 all-gather.6
  364.2 10.2 all-gather.8
  375.8 10.1 all-gather.10
where the time goes:
time: 856 us; the launch traced here: 842 us
  local copies, waits for them, and re-layouts  390 us (46%)
  other arithmetic  217 us (25%)
  matrix products  128 us (15%)
  starting transfers between devices  50.1 us (6%)
  waiting for transfers between devices  37.9 us (4%)
  between operations  15 us (2%)
    unnamed x139, local copies, waits for them, and re-layouts  194 us
    unnamed x12, other arithmetic  180 us
    transpose x4, local copies, waits for them, and re-layouts, from_halves(): array.transpose(0, 2, 1, 3)  74.4 us
    reshape x4, local copies, waits for them, and re-layouts, from_halves(): array.transpose(0, 2, 1, 3)  46.8 us
    dot_general x4, matrix products, body(): jnp.einsum('shqd,shkd->shqk', grad_part, value_part, preferred_element_ty...  27.2 us
    reshape x8, local copies, waits for them, and re-layouts, to_halves(): array.reshape(2, total_rows // 2, head_count, DH).transpose(0, 2, 1, 3)  25.9 us
    dot_general x5, matrix products, scaled_scores(): jnp.einsum('shqd,shkd->shqk', query_part, key_part, preferred_element_typ...  23.6 us
    dot_general x4, matrix products, body(): jnp.einsum('shqk,shkd->shqd', weights_low, value_part, preferred_element_...  23.5 us
  transfers between devices with their start and end apart: 12, of which 3 were waited for; matrix products, arithmetic and copies ran while one was open for 72% of the time, Pallas kernels for 0%

commit v1 on v0

v1 whole, which is shorter than its diff:
```python
import functools

import jax
import jax.numpy as jnp
from jax import lax
from jax.experimental import pallas as pl
from jax.experimental.pallas import tpu as pltpu
from jax.sharding import PartitionSpec as P

DH = 128
DOC_MOST = 512
QUERY_ROWS = 256
SCALE = DH ** (-0.5)
LOG2E = 1.4426950408889634
NEG_LARGE = -1e30
MESH = pl.DeviceIdType.MESH


def dot(a, b, a_dim, b_dim):
    return lax.dot_general(
        a, b, (((a_dim,), (b_dim,)), ((), ())), preferred_element_type=jnp.float32
    )


def wait_bytes(ref, sem):
    pltpu.make_async_copy(ref, ref, sem).wait()


def attend_block(refs, h, half, block, rows):
    qx, gx, kx, vx, first_ref, yout, key_acc, value_acc = refs
    window = DOC_MOST + rows
    low = pl.multiple_of(block * rows, rows)
    half_rows = qx.shape[2]
    q = qx[h, half, pl.ds(low, rows), :]
    g = gx[h, half, pl.ds(low, rows), :]
    k = kx[h, half, pl.ds(low, window), :]
    v = vx[h, half, pl.ds(low, window), :]
    scores = dot(k, q, 1, 1)
    prob_grad = dot(v, g, 1, 1)
    key_row = lax.broadcasted_iota(jnp.int32, (window, rows), 0)
    query_row = lax.broadcasted_iota(jnp.int32, (window, rows), 1)
    visible = (key_row >= first_ref[half, block] - (low - DOC_MOST)) & (
        key_row - query_row <= DOC_MOST
    )
    scores = jnp.where(visible, scores * (SCALE * LOG2E), NEG_LARGE)
    top = jnp.max(scores, axis=0, keepdims=True)
    mass = jnp.exp2(scores - top)
    weights = mass * (1.0 / jnp.sum(mass, axis=0, keepdims=True))
    weights_low = weights.astype(jnp.bfloat16)
    attended = dot(v, weights_low, 0, 0)
    attended_low = attended.astype(jnp.bfloat16).astype(jnp.float32)
    grad_turned = g.astype(jnp.float32).T
    delta = jnp.sum(attended_low * grad_turned, axis=0, keepdims=True)
    score_grad = (weights * (prob_grad - delta)).astype(jnp.bfloat16)
    query_grad = dot(k, score_grad, 0, 0) * SCALE
    out_rows = pl.ds(half * half_rows + low, rows)
    yout[0, h, out_rows, :] = attended.T.astype(jnp.bfloat16)
    yout[1, h, out_rows, :] = query_grad.T.astype(jnp.bfloat16)
    key_acc[half, pl.ds(low, window), :] += dot(score_grad, q, 1, 0)
    value_acc[half, pl.ds(low, window), :] += dot(weights_low, g, 1, 0)


def kernel(
    sizes,
    slots_ref, first_ref, q_hbm, k_hbm, v_hbm, g_hbm,
    o_out, dq_out, dk_out, dv_out,
    qx, kx, vx, gx, tails, stage, parts, yout, key_acc, value_acc,
    in_send, in_recv, tail_send, tail_recv, part_send, part_recv, out_send, out_recv,
):
    inner, group, outer, heads = sizes
    rows = q_hbm.shape[1]
    half_rows = qx.shape[2]
    in_half = group // 2
    me = lax.axis_index("head") * inner + lax.axis_index("inner")
    rank = lax.axis_index("outer")
    query_rows = first_ref.shape[3]
    blocks = half_rows // query_rows

    def peer_of(step):
        return lax.rem(me + step, group)

    def group_id(peer):
        return {"head": peer // inner, "inner": lax.rem(peer, inner)}

    def rank_of(step):
        return lax.rem(rank + step, outer)

    barrier = pltpu.get_barrier_semaphore()

    def greet(step, carry):
        pl.semaphore_signal(barrier, inc=1, device_id=group_id(peer_of(step)), device_id_type=MESH)
        return carry

    lax.fori_loop(1, group, greet, 0)
    for step in range(1, outer):
        pl.semaphore_signal(
            barrier, inc=1, device_id={"outer": rank_of(step)}, device_id_type=MESH
        )
    pl.semaphore_wait(barrier, group - 1 + outer - 1)

    my_half = me // in_half
    my_low = pl.multiple_of(lax.rem(me, in_half) * rows, rows)
    arrays = (
        (k_hbm, kx, DOC_MOST),
        (v_hbm, vx, DOC_MOST),
        (q_hbm, qx, 0),
        (g_hbm, gx, 0),
    )
    outs = (o_out, dq_out, dk_out, dv_out)

    def columns(owner, h):
        return pl.ds(pl.multiple_of((owner * heads + h) * DH, DH), DH)

    for h in range(heads):
        for a, (src, dst, skip) in enumerate(arrays):
            pltpu.make_async_copy(
                src.at[0, :, columns(me, h)],
                dst.at[h, my_half, pl.ds(my_low + skip, rows), :],
                in_recv.at[a, h],
            ).start()

        def send_in(step, carry):
            peer = peer_of(step)
            for a, (src, dst, skip) in enumerate(arrays):
                pltpu.make_async_remote_copy(
                    src_ref=src.at[0, :, columns(peer, h)],
                    dst_ref=dst.at[h, my_half, pl.ds(my_low + skip, rows), :],
                    send_sem=in_send.at[a, h],
                    recv_sem=in_recv.at[a, h],
                    device_id=group_id(peer),
                    device_id_type=MESH,
                ).start()
            return carry

        lax.fori_loop(1, group, send_in, 0)

    def send_out(a, h):
        pltpu.make_async_copy(
            yout.at[a, h, pl.ds(pl.multiple_of(me * rows, rows), rows), :],
            outs[a].at[0, :, columns(me, h)],
            out_recv.at[a],
        ).start()

        def send_one(step, carry):
            peer = peer_of(step)
            pltpu.make_async_remote_copy(
                src_ref=yout.at[a, h, pl.ds(pl.multiple_of(peer * rows, rows), rows), :],
                dst_ref=outs[a].at[0, :, columns(me, h)],
                send_sem=out_send.at[a, h],
                recv_sem=out_recv.at[a],
                device_id=group_id(peer),
                device_id_type=MESH,
            ).start()
            return carry

        lax.fori_loop(1, group, send_one, 0)

    own_slots = pl.ds(2 * rank, 2)
    far_slots = pl.ds(0, 2 * (outer - 1))
    accs = (key_acc, value_acc)
    refs = (qx, gx, kx, vx, first_ref, yout, key_acc, value_acc)
    for h in range(heads):
        for a, (_, dst, skip) in enumerate(arrays):
            wait_bytes(dst.at[h, :, pl.ds(skip, half_rows), :], in_recv.at[a, h])
        for a, ext in enumerate((kx, vx)):
            tail = ext.at[h, :, pl.ds(half_rows, DOC_MOST), :]
            pltpu.make_async_copy(tail, tails[a][h].at[own_slots], tail_recv.at[a, h]).start()
            for step in range(1, outer):
                pltpu.make_async_remote_copy(
                    src_ref=tail,
                    dst_ref=tails[a][h].at[own_slots],
                    send_sem=tail_send.at[a, h],
                    recv_sem=tail_recv.at[a, h],
                    device_id={"outer": rank_of(step)},
                    device_id_type=MESH,
                ).start()
        key_acc[...] = jnp.zeros_like(key_acc)
        value_acc[...] = jnp.zeros_like(value_acc)
        near = min(DOC_MOST // query_rows, blocks)

        def attend(block, carry):
            for half in range(2):
                attend_block(refs, h, half, block, query_rows)
            return carry

        lax.fori_loop(near, blocks, attend, 0)
        for a, ext in enumerate((kx, vx)):
            wait_bytes(tails[a][h], tail_recv.at[a, h])
            for half in range(2):
                ext[h, half, pl.ds(0, DOC_MOST), :] = tails[a][h][slots_ref[half]]
        lax.fori_loop(0, near, attend, 0)
        for a in range(2):
            send_out(a, h)
        for a, acc in enumerate(accs):
            stage[a, h] = acc[:, pl.ds(0, DOC_MOST), :].astype(stage.dtype)
            pltpu.make_async_copy(
                stage.at[a, h], parts[a][h].at[own_slots], part_recv.at[a, h]
            ).start()
            for step in range(1, outer):
                pltpu.make_async_remote_copy(
                    src_ref=stage.at[a, h],
                    dst_ref=parts[a][h].at[own_slots],
                    send_sem=part_send.at[a, h],
                    recv_sem=part_recv.at[a, h],
                    device_id={"outer": rank_of(step)},
                    device_id_type=MESH,
                ).start()
        for a, acc in enumerate(accs):
            factor = SCALE if a == 0 else 1.0
            wait_bytes(parts[a][h], part_recv.at[a, h])
            for half in range(2):
                start = half * half_rows
                bulk = half_rows - DOC_MOST
                part = parts[a][h][slots_ref[2 + half]].astype(jnp.float32)
                part = jnp.where(slots_ref[4 + half] > 0, part, 0.0)
                yout[2 + a, h, pl.ds(start, bulk), :] = (
                    acc[half, pl.ds(DOC_MOST, bulk), :] * factor
                ).astype(jnp.bfloat16)
                yout[2 + a, h, pl.ds(start + bulk, DOC_MOST), :] = (
                    (acc[half, pl.ds(half_rows, DOC_MOST), :] + part) * factor
                ).astype(jnp.bfloat16)
            send_out(2 + a, h)

    others = pl.ds(0, (group - 1) * rows)
    for h in range(heads):
        for a in range(4):
            wait_bytes(yout.at[a, h, others, :], in_send.at[a, h])
            wait_bytes(yout.at[a, h, others, :], out_send.at[a, h])
        if outer > 1:
            for a in range(2):
                wait_bytes(tails[a][h].at[far_slots], tail_send.at[a, h])
                wait_bytes(parts[a][h].at[far_slots], part_send.at[a, h])
    for a in range(4):
        wait_bytes(outs[a], out_recv.at[a])


def slot_of(span_ids, wanted):
    slot_ids = jnp.arange(span_ids.shape[0], dtype=jnp.int32)
    return jnp.sum(jnp.where(span_ids[None, :] == wanted[:, None], slot_ids[None, :], 0), axis=1)


def body(sizes, queries, key_states, value_states, out_grad, positions, doc_start):
    inner, group, outer, heads = sizes
    total_rows = positions.shape[1]
    half_rows = total_rows // 2
    query_rows = min(QUERY_ROWS, half_rows)
    slots = 2 * outer
    pos_table = positions.reshape(slots, half_rows)
    span_ids = pos_table[:, 0] // half_rows
    own_slots = lax.axis_index("outer") * 2 + jnp.arange(2, dtype=jnp.int32)
    span_here = jnp.take(span_ids, own_slots)
    first = jnp.take(doc_start.reshape(slots, half_rows), own_slots, axis=0)
    first = (first - span_here[:, None] * half_rows).reshape(2, half_rows // query_rows, 1, query_rows)
    slot_table = jnp.concatenate(
        [
            slot_of(span_ids, span_here - 1),
            slot_of(span_ids, span_here + 1),
            (span_here + 1 < slots).astype(jnp.int32),
            jnp.zeros((2,), jnp.int32),
        ]
    )
    ext_rows = DOC_MOST + half_rows
    low = jnp.bfloat16
    per_head = [[pltpu.VMEM((slots, DOC_MOST, DH), low)] * heads] * 2
    any_spec = pl.BlockSpec(memory_space=pl.ANY)
    dma = pltpu.SemaphoreType.DMA
    return pl.pallas_call(
        functools.partial(kernel, sizes),
        out_shape=[jax.ShapeDtypeStruct(queries.shape, low)] * 4,
        in_specs=[
            pl.BlockSpec(memory_space=pltpu.SMEM),
            pl.BlockSpec(memory_space=pltpu.VMEM),
        ]
        + [any_spec] * 4,
        out_specs=[any_spec] * 4,
        scratch_shapes=[
            pltpu.VMEM((heads, 2, half_rows, DH), low),
            pltpu.VMEM((heads, 2, ext_rows, DH), low),
            pltpu.VMEM((heads, 2, ext_rows, DH), low),
            pltpu.VMEM((heads, 2, half_rows, DH), low),
            per_head,
            pltpu.VMEM((2, heads, 2, DOC_MOST, DH), low),
            per_head,
            pltpu.VMEM((4, heads, total_rows, DH), low),
            pltpu.VMEM((2, ext_rows, DH), jnp.float32),
            pltpu.VMEM((2, ext_rows, DH), jnp.float32),
            dma((4, heads)),
            dma((4, heads)),
            dma((2, heads)),
            dma((2, heads)),
            dma((2, heads)),
            dma((2, heads)),
            dma((4, heads)),
            dma((4,)),
        ],
        compiler_params=pltpu.CompilerParams(
            collective_id=0, has_side_effects=True, vmem_limit_bytes=56 * 2**20
        ),
    )(slot_table, first, queries, key_states, value_states, out_grad)


def solution(mesh):
    group = mesh.shape["head"] * mesh.shape["inner"]
    outer = mesh.shape["outer"]

    def run(queries, *rest):
        heads = queries.shape[2] // DH // group
        sizes = (mesh.shape["inner"], group, outer, heads)
        spec = P("outer", ("head", "inner"), None)
        return jax.shard_map(
            lambda *args: tuple(body(sizes, *args)),
            mesh=mesh,
            in_specs=(spec, spec, spec, spec, P(), P()),
            out_specs=(spec, spec, spec, spec),
            check_vma=False,
        )(queries, *rest)

    return run
```

time: 856 us -> 391 us (0.46); the launches traced: 842 us -> 390 us
  local copies, waits for them, and re-layouts: 390 us -> 12.2 us
  Pallas kernels: 0 us -> 376 us
  other arithmetic: 217 us -> 1.54 us
  matrix products: 128 us -> 0 us
  starting transfers between devices: 50.1 us -> 0 us
  waiting for transfers between devices: 37.9 us -> 0 us
  between operations: 15 us -> 0.71 us
    pallas_call x0 -> x1, Pallas kernels: none -> 376 us  [body(): pl.pallas_call(functools.partial(kernel, sizes), out_shape=[jax.ShapeDtyp...]
    unnamed x139 -> x11, local copies, waits for them, and re-layouts: 194 us -> 9.39 us
    unnamed x12 -> x0, other arithmetic: 180 us -> none
    dot_general x27 -> x0, matrix products: 128 us -> none  [the longest x4 27.2 us: body(): jnp.einsum('shqd,shkd->shqk', grad_part, value_part, preferred_element_ty...]
    transpose x4 -> x0, local copies, waits for them, and re-layouts: 74.4 us -> none  [from_halves(): array.transpose(0, 2, 1, 3)]
    reshape x14 -> x2, local copies, waits for them, and re-layouts: 72.7 us -> 1.58 us  [the longest x1 0.79 us: body(): pos_table = positions.reshape(slots, half_rows)]
    all_to_all x8 -> x0, starting transfers between devices: 49.7 us -> none  [the longest x1 8.31 us: body(): lax.all_to_all(key_states, ('head', 'inner'), split_axis=2, concat_axis=1...]
    all_to_all x8 -> x0, waiting for transfers between devices: 37.7 us -> none  [the longest x1 13 us: body(): lax.all_to_all(key_states, ('head', 'inner'), split_axis=2, concat_axis=1...]
  transfers between devices with their start and end apart: 12 -> 0, of which waited for: 3 -> 0; matrix products, arithmetic and copies ran while one was open for 72% -> 0% of each run, Pallas kernels for 0% -> 0%
where the time goes in v1:
time: 391 us; the launch traced here: 390 us
  Pallas kernels  376 us (96%)
  local copies, waits for them, and re-layouts  12.2 us (3%)
    pallas_call x1, Pallas kernels, body(): pl.pallas_call(functools.partial(kernel, sizes), out_shape=[jax.ShapeDtyp...  376 us
    unnamed x11, local copies, waits for them, and re-layouts  9.39 us

profile of v1, /device:TPU:0, one launch (start us, length us, event | category | flops | bytes accessed | tf_op | source)
XLA Modules:
  0.0 390.1 jit_solution(16406364706073173129)
XLA Ops:
  0.7 0.8 reshape.106
  1.5 0.1 copy.13
  1.6 0.6 gather_fusion
  2.3 0.2 fusion.1
  2.5 0.6 pad_add_fusion.slots_ref
  3.1 0.8 reshape.107
  3.9 0.6 gather_fusion.1
  4.5 0.7 fusion.first_ref
  5.2 375.7 %shard_map.93 = (bf16[1,256,4096]{2,1,0:T(8,128)(2,1)}, bf16[1,256,4096]{2,1,0:T(8,128)(2,1)}, bf16[1,256,4096]{2,1,0:T(8,128)(2,1)}, bf16[1,256,4096]{2,1,0:T(8,128)(2,1)}) custom-call(s32[8]{0:T(128)} %pad_add_fusion.slots_ref, s32[2,8,1,256]{3,2,1,0:T(1,128)} %fusion.first_ref, bf16[1,256,4096]{2,1,0:T(8,128)(2,1)} %q_hbm.1, bf16[1,256,4096]{2,1,0:T(8,128)(2,1)} %k_hbm.1, ...), custom_call_target="tpu_custom_call" | custom-call | tf_op jit(solution)/shard_map/pallas_call | solution.py:267
  380.8 0.0 copy-start.2
  380.8 3.3 copy.18
  384.1 0.0 copy-done.2
  384.1 0.0 copy-start.1
  384.1 1.3 copy.19
  385.4 1.0 copy-done.1
  386.5 0.0 copy-start
  386.5 1.3 copy.20
  387.8 1.0 copy-done
  388.8 1.3 copy.21
  (10 shorter events, 0.1 us)
Async XLA Ops:
  380.8 3.3 copy-start.2
  384.1 2.3 copy-start.1
  386.5 2.3 copy-start

commit v2 on v1

--- a/solution.py
+++ b/solution.py
@@ -26,7 +26,7 @@
     pltpu.make_async_copy(ref, ref, sem).wait()
 
 
-def attend_block(refs, h, half, block, rows):
+def attend_block(refs, h, half, block, rows, rank, base):
     qx, gx, kx, vx, first_ref, yout, key_acc, value_acc = refs
     window = DOC_MOST + rows
     low = pl.multiple_of(block * rows, rows)
@@ -39,7 +39,8 @@
     prob_grad = dot(v, g, 1, 1)
     key_row = lax.broadcasted_iota(jnp.int32, (window, rows), 0)
     query_row = lax.broadcasted_iota(jnp.int32, (window, rows), 1)
-    visible = (key_row >= first_ref[half, block] - (low - DOC_MOST)) & (
+    first = first_ref[pl.ds(rank, 1), pl.ds(pl.multiple_of(half * half_rows + low, rows), rows)]
+    visible = (key_row >= first - (base + low - DOC_MOST)) & (
         key_row - query_row <= DOC_MOST
     )
     scores = jnp.where(visible, scores * (SCALE * LOG2E), NEG_LARGE)
@@ -62,7 +63,7 @@
 
 def kernel(
     sizes,
-    slots_ref, first_ref, q_hbm, k_hbm, v_hbm, g_hbm,
+    pos_ref, first_ref, q_hbm, k_hbm, v_hbm, g_hbm,
     o_out, dq_out, dk_out, dv_out,
     qx, kx, vx, gx, tails, stage, parts, yout, key_acc, value_acc,
     in_send, in_recv, tail_send, tail_recv, part_send, part_recv, out_send, out_recv,
@@ -73,11 +74,11 @@
     in_half = group // 2
     me = lax.axis_index("head") * inner + lax.axis_index("inner")
     rank = lax.axis_index("outer")
-    query_rows = first_ref.shape[3]
+    query_rows = min(QUERY_ROWS, half_rows)
     blocks = half_rows // query_rows
 
     def peer_of(step):
-        return lax.rem(me + step, group)
+        return lax.rem(me + 1 + lax.rem(step - 1 + (group // 2 - 1) * rank, group - 1), group)
 
     def group_id(peer):
         return {"head": peer // inner, "inner": lax.rem(peer, inner)}
@@ -85,6 +86,18 @@
     def rank_of(step):
         return lax.rem(rank + step, outer)
 
+    slots = 2 * outer
+    bases = [pos_ref[rank, half * half_rows] for half in range(2)]
+
+    def slot_at(wanted):
+        found = jnp.int32(0)
+        for slot in range(slots):
+            start = pos_ref[slot // 2, (slot % 2) * half_rows]
+            found = jnp.where(start == wanted, jnp.int32(slot), found)
+        return found
+
+    prev_slots = [slot_at(base - half_rows) for base in bases]
+    next_slots = [slot_at(base + half_rows) for base in bases]
     barrier = pltpu.get_barrier_semaphore()
 
     def greet(step, carry):
@@ -133,6 +146,9 @@
             return carry
 
         lax.fori_loop(1, group, send_in, 0)
+        if h + 1 < heads:
+            for a in range(4):
+                wait_bytes(yout.at[a, h, pl.ds(0, (group - 1) * rows), :], in_send.at[a, h])
 
     def send_out(a, h):
         pltpu.make_async_copy(
@@ -180,14 +196,14 @@
 
         def attend(block, carry):
             for half in range(2):
-                attend_block(refs, h, half, block, query_rows)
+                attend_block(refs, h, half, block, query_rows, rank, bases[half])
             return carry
 
         lax.fori_loop(near, blocks, attend, 0)
         for a, ext in enumerate((kx, vx)):
             wait_bytes(tails[a][h], tail_recv.at[a, h])
             for half in range(2):
-                ext[h, half, pl.ds(0, DOC_MOST), :] = tails[a][h][slots_ref[half]]
+                ext[h, half, pl.ds(0, DOC_MOST), :] = tails[a][h][prev_slots[half]]
         lax.fori_loop(0, near, attend, 0)
         for a in range(2):
             send_out(a, h)
@@ -211,8 +227,8 @@
             for half in range(2):
                 start = half * half_rows
                 bulk = half_rows - DOC_MOST
-                part = parts[a][h][slots_ref[2 + half]].astype(jnp.float32)
-                part = jnp.where(slots_ref[4 + half] > 0, part, 0.0)
+                part = parts[a][h][next_slots[half]].astype(jnp.float32)
+                part = jnp.where(bases[half] + half_rows < slots * half_rows, part, 0.0)
                 yout[2 + a, h, pl.ds(start, bulk), :] = (
                     acc[half, pl.ds(DOC_MOST, bulk), :] * factor
                 ).astype(jnp.bfloat16)
@@ -224,7 +240,8 @@
     others = pl.ds(0, (group - 1) * rows)
     for h in range(heads):
         for a in range(4):
-            wait_bytes(yout.at[a, h, others, :], in_send.at[a, h])
+            if h + 1 == heads:
+                wait_bytes(yout.at[a, h, others, :], in_send.at[a, h])
             wait_bytes(yout.at[a, h, others, :], out_send.at[a, h])
         if outer > 1:
             for a in range(2):
@@ -234,31 +251,11 @@
         wait_bytes(outs[a], out_recv.at[a])
 
 
-def slot_of(span_ids, wanted):
-    slot_ids = jnp.arange(span_ids.shape[0], dtype=jnp.int32)
-    return jnp.sum(jnp.where(span_ids[None, :] == wanted[:, None], slot_ids[None, :], 0), axis=1)
-
-
 def body(sizes, queries, key_states, value_states, out_grad, positions, doc_start):
     inner, group, outer, heads = sizes
     total_rows = positions.shape[1]
     half_rows = total_rows // 2
-    query_rows = min(QUERY_ROWS, half_rows)
     slots = 2 * outer
-    pos_table = positions.reshape(slots, half_rows)
-    span_ids = pos_table[:, 0] // half_rows
-    own_slots = lax.axis_index("outer") * 2 + jnp.arange(2, dtype=jnp.int32)
-    span_here = jnp.take(span_ids, own_slots)
-    first = jnp.take(doc_start.reshape(slots, half_rows), own_slots, axis=0)
-    first = (first - span_here[:, None] * half_rows).reshape(2, half_rows // query_rows, 1, query_rows)
-    slot_table = jnp.concatenate(
-        [
-            slot_of(span_ids, span_here - 1),
-            slot_of(span_ids, span_here + 1),
-            (span_here + 1 < slots).astype(jnp.int32),
-            jnp.zeros((2,), jnp.int32),
-        ]
-    )
     ext_rows = DOC_MOST + half_rows
     low = jnp.bfloat16
     per_head = [[pltpu.VMEM((slots, DOC_MOST, DH), low)] * heads] * 2
@@ -296,7 +293,7 @@
         compiler_params=pltpu.CompilerParams(
             collective_id=0, has_side_effects=True, vmem_limit_bytes=56 * 2**20
         ),
-    )(slot_table, first, queries, key_states, value_states, out_grad)
+    )(positions, doc_start, queries, key_states, value_states, out_grad)
 
 
 def solution(mesh):

time: 391 us -> 381 us (0.974)
  Pallas kernels: 376 us -> 370 us
    pallas_call x1, Pallas kernels: 376 us -> 370 us  [body(): pl.pallas_call(functools.partial(kernel, sizes), out_shape=[jax.ShapeDtyp...]
    unnamed x11 -> x10, local copies, waits for them, and re-layouts: 9.39 us -> 9.29 us
where the time goes in v2:
time: 381 us; the launch traced here: 380 us
  Pallas kernels  370 us (97%)
  local copies, waits for them, and re-layouts  9.29 us (2%)
    pallas_call x1, Pallas kernels, body(): pl.pallas_call(functools.partial(kernel, sizes), out_shape=[jax.ShapeDtyp...  370 us
    unnamed x10, local copies, waits for them, and re-layouts  9.29 us

profile of v2, /device:TPU:0, one launch (start us, length us, event | category | flops | bytes accessed | tf_op | source)
XLA Modules:
  0.0 380.3 jit_solution(9179708097004558773)
XLA Ops:
  0.6 370.4 %shard_map.93 = (bf16[1,256,4096]{2,1,0:T(8,128)(2,1)}, bf16[1,256,4096]{2,1,0:T(8,128)(2,1)}, bf16[1,256,4096]{2,1,0:T(8,128)(2,1)}, bf16[1,256,4096]{2,1,0:T(8,128)(2,1)}) custom-call(s32[2,4096]{1,0:T(2,128)} %pos_ref.1, s32[2,4096]{1,0:T(2,128)} %first_ref.1, bf16[1,256,4096]{2,1,0:T(8,128)(2,1)} %q_hbm.1, bf16[1,256,4096]{2,1,0:T(8,128)(2,1)} %k_hbm.1, ...), custom_call_target="tpu_custom_call" | custom-call | tf_op jit(solution)/shard_map/pallas_call | solution.py:264
  371.0 0.0 copy-start.2
  371.0 3.3 copy.14
  374.3 0.0 copy-done.2
  374.3 0.0 copy-start.1
  374.3 1.3 copy.15
  375.6 1.0 copy-done.1
  376.6 0.0 copy-start
  376.6 1.3 copy.16
  378.0 1.0 copy-done
  379.0 1.3 copy.17
Async XLA Ops:
  371.0 3.3 copy-start.2
  374.3 2.3 copy-start.1
  376.6 2.3 copy-start
